TPU v7x, 32 devices: a whole 2x2x4 slice. The times are simulated.
32 devices in a mesh: axial: 16 (over z, y, core), circ: 2 (over x).
Axes of the slice: x: 2, y: 2, z: 4, core: 2. Of those that a mesh axis runs over, the one named last changes fastest.
Arguments:
- mode_shapes: float32 [32, 4, 128, 512], P('axial', 'circ'), may hold values from -0.0625 to 0.0625
- amplitude: float32 [32, 4, 128], P('axial', 'circ'), may hold values from 0.3 to 3
- pair_list: int32 [16, 2, 3, 20], P('axial', 'circ'), may hold values from -1 to 3, as said below
- pair_counts: int32 [16, 2], P('axial', 'circ'), may hold values from 2 to 20, as said below
Outputs:
- modal_spectrum: float32 [2, 512, 512], P(None, 'axial', 'circ')
Inputs may be any that keep to these rules, and one draw needn't show every extreme that they name: `pair_list`: each device's 20 slots hold distinct pairs, and each of its local blocks is the row block of exactly five slots, one for each of the five offsets. Entry 0 is the row block's local index i * 2 + j of the device's 2 x 2 blocks, entry 1 the axial offset (0 or 1), entry 2 the circumferential offset (-1, 0 or 1), and an axial offset 0 comes only with a circumferential offset of 0 or 1. `pair_counts`: some device keeps all 20 slots.
All inputs are finite; a program needn't handle non-finite values.
Results may differ from a plain program's by a relative error of at most 0.0022.
Values may be sent and summed in bfloat16 or wider, within the bound.
A program may use at most 64 MiB of HBM per device.

v0:
```python
import jax
import jax.numpy as jnp
from jax import lax
from jax.sharding import PartitionSpec as P

ALONG = 16
AROUND = 8


axial_decay = 0.125
circ_decay = 0.16
wavenumber = 0.6


def with_halo(block, sides, width):
    for axis, dim in sides:
        count = lax.axis_size(axis)
        forward = [(i, i + 1) for i in range(count - 1)]
        forward.append((count - 1, 0))
        backward = [(target, source) for source, target in forward]
        low = lax.ppermute(
            lax.slice_in_dim(block, block.shape[dim] - width, None, axis=dim), axis, forward
        )
        high = lax.ppermute(lax.slice_in_dim(block, 0, width, axis=dim), axis, backward)
        block = jnp.concatenate([low, block, high], axis=dim)
    return block


def from_behind(block, axis, distance):
    devices = range(lax.axis_size(axis))
    route = [(i - distance, i) for i in devices if i - distance in devices]
    return lax.ppermute(block, axis, route)


def corcos_tiles(step_along, step_around, weight):
    patch_index = jnp.arange(ALONG * AROUND, dtype=jnp.int32)
    along_pos = (patch_index // AROUND).astype(jnp.float32)
    around_pos = (patch_index % AROUND).astype(jnp.float32)
    gap_along = (
        step_along.astype(jnp.float32)[:, None, None] * ALONG
        + along_pos[None, None, :]
        - along_pos[None, :, None]
    )
    gap_around = (
        step_around.astype(jnp.float32)[:, None, None] * AROUND
        + around_pos[None, None, :]
        - around_pos[None, :, None]
    )
    envelope = weight[:, None, None] * jnp.exp(
        -axial_decay * jnp.abs(gap_along) - circ_decay * jnp.abs(gap_around)
    )
    real_tile = envelope * jnp.cos(wavenumber * gap_along)
    imag_tile = -envelope * jnp.sin(wavenumber * gap_along)
    return jnp.stack([real_tile, imag_tile], axis=1).astype(jnp.bfloat16)


def slot_products(chosen, slot_index, pair_total, flattened, around_blocks):
    row_block = chosen[0]
    step_along = chosen[1]
    step_around = chosen[2]
    valid = (slot_index < pair_total).astype(jnp.float32)
    weight = valid * jnp.where((step_along == 0) & (step_around == 0), 0.5, 1.0).astype(jnp.float32)
    column = (
        (row_block // around_blocks + step_along) * (around_blocks + 2)
        + row_block % around_blocks
        + step_around
        + 1
    )
    columns = flattened[column]
    tiles = corcos_tiles(step_along, step_around, weight)
    return jnp.einsum("pcij,pjm->picm", tiles, columns, preferred_element_type=jnp.float32)


def body(mode_shapes, amplitude, pair_list, pair_counts):
    along_blocks, around_blocks, patch_count, mode_count = mode_shapes.shape
    block_count = along_blocks * around_blocks
    weighted = (mode_shapes * amplitude[..., None]).astype(jnp.bfloat16)
    widened = with_halo(weighted, (("circ", 1),), 1)
    ahead_rows = from_behind(widened[:1], "axial", -1)
    extended = jnp.concatenate([widened, ahead_rows], axis=0)
    flattened = extended.reshape((along_blocks + 1) * (around_blocks + 2), patch_count, mode_count)
    listing = pair_list[0, 0]
    pair_total = pair_counts[0, 0]
    slot_total = listing.shape[1]
    group_size = 5 * around_blocks
    group_count = slot_total // group_size
    empty = jnp.zeros((block_count, patch_count, 2 * mode_count), jnp.float32)
    sort_keys = listing[0] * slot_total + jnp.arange(slot_total, dtype=jnp.int32)
    ordering = jnp.argsort(sort_keys)
    ordered = listing[:, ordering]

    def add_row(index, totals):
        chosen = lax.dynamic_slice_in_dim(ordered, index * group_size, group_size, 1)
        slot_index = lax.dynamic_slice_in_dim(ordering, index * group_size, group_size, 0)
        products = slot_products(chosen, slot_index, pair_total, flattened, around_blocks)
        summed = jnp.sum(products.reshape(around_blocks, 5, patch_count, 2 * mode_count), axis=1)
        return lax.dynamic_update_slice_in_dim(totals, summed, index * around_blocks, 0)

    row_sums = lax.fori_loop(0, group_count, add_row, empty)
    rounded = row_sums.astype(jnp.bfloat16).reshape(block_count * patch_count, 2 * mode_count)
    local = weighted.reshape(block_count * patch_count, mode_count)
    cross = lax.dot_general(
        local, rounded, (((0,), (0,)), ((), ())), preferred_element_type=jnp.float32
    )
    real_part = cross[:, :mode_count]
    imag_part = cross[:, mode_count:]
    summand = jnp.stack([real_part + real_part.T, imag_part - imag_part.T])
    partial_value = lax.psum_scatter(summand, "axial", scatter_dimension=1, tiled=True)
    result = lax.psum_scatter(partial_value, "circ", scatter_dimension=2, tiled=True)
    return result


def solution(mesh):
    in_specs = (
        P("axial", "circ", None, None),
        P("axial", "circ", None),
        P("axial", "circ", None, None),
        P("axial", "circ"),
    )
    out_specs = P(None, "axial", "circ")
    return jax.shard_map(body, mesh=mesh, in_specs=in_specs, out_specs=out_specs, check_vma=False)
```

profile of v0, /device:TPU:0, one launch (start us, length us, event | category | flops | bytes accessed | tf_op | source)
XLA Modules:
  0.0 153.8 jit_solution(13101074092874906572)
XLA Ops:
  6.5 0.0 reduce-scatter.3.cloned.1.call-start
  6.5 1.4 multiply_convert_fusion
  8.0 3.0 %collective-permute-start = (bf16[2,1,128,512]{3,2,1,0:T(8,128)(2,1)S(1)}, bf16[2,1,128,512]{3,2,1,0:T(8,128)(2,1)S(1)}, u32[]{:S(2)}, u32[]{:S(2)}) collective-permute-start(bf16[2,1,128,512]{3,2,1,0:T(8,128)(2,1)S(1)} %get-tuple-element.241), channel_id=1, source_target_pairs={{0,1},{1,0},{2,3},{3,2},{4,5},{5,4},{6,7},{7,6},{8,9},{9,8},{10,11... | collective-permute-start | bytes 786440 | tf_op jit(solution)/shard_map/ppermute | solution.py:21
  11.0 0.1 collective-permute-start.1
  11.0 0.0 copy-done
  11.0 0.1 copy.27
  11.1 7.0 %collective-permute-done = bf16[2,1,128,512]{3,2,1,0:T(8,128)(2,1)S(1)} collective-permute-done((bf16[2,1,128,512]{3,2,1,0:T(8,128)(2,1)S(1)}, bf16[2,1,128,512]{3,2,1,0:T(8,128)(2,1)S(1)}, u32[]{:S(2)}, u32[]{:S(2)}) %collective-permute-start) | collective-permute-done | bytes 262176 | tf_op jit(solution)/shard_map/ppermute | solution.py:21
  18.1 4.8 %collective-permute-done.1 = bf16[2,1,128,512]{3,2,1,0:T(8,128)(2,1)S(1)} collective-permute-done((bf16[2,1,128,512]{3,2,1,0:T(8,128)(2,1)S(1)}, bf16[2,1,128,512]{3,2,1,0:T(8,128)(2,1)S(1)}, u32[]{:S(2)}, u32[]{:S(2)}) %collective-permute-start.1) | collective-permute-done | bytes 262176 | tf_op jit(solution)/shard_map/ppermute | solution.py:24
  22.9 0.1 pad_maximum_fusion.2
  23.0 1.3 collective-permute-start.2
  24.3 1.6 %sort.17 = (s32[20]{0:T(128)}, s32[20]{0:T(128)S(1)}) sort(s32[20]{0:T(128)S(1)} %bitcast_add_fusion.2, s32[20]{0:T(128)S(1)} %iota.49), dimensions={0}, to_apply=%region_0.0 | sort | flops 100 | bytes 320 | tf_op jit(solution)/shard_map/jit(argsort)/sort | solution.py:89
  25.9 0.6 gather_fusion.1
  26.5 0.1 copy.19
  26.6 0.2 collective-permute-done.2
  26.8 0.2 pad_maximum_fusion.1
  27.0 1.1 broadcast_in_dim.55.clone
  28.1 26.6 %while.16 = (s32[]{:T(128)}, bf16[4,128,1024]{2,1,0:T(8,128)(2,1)}, s32[3,20]{1,0:T(4,128)S(1)}, bf16[12,128,512]{2,1,0:T(8,128)(2,1)S(1)}, s32[20]{0:T(128)S(1)...) while((s32[]{:T(128)}, bf16[4,128,1024]{2,1,0:T(8,128)(2,1)}, ...), condition=%wide.region_3.4_spmd, body=%wide.region_1.3_spmd.sunk | while | flops 340203136 | bytes 18378884 | solution.py:99
  28.1 0.1 constant_dynamic-slice_fusion.2
  28.2 0.7 compare_select_fusion.7
  28.9 0.1 broadcast_add_fusion.4
  29.0 0.1 broadcast_add_fusion.5
  29.1 3.5 %fusion.39 = (bf16[10,1,128,128]{3,2,1,0:T(8,128)(2,1)}, bf16[10,1,128,128]{3,2,1,0:T(8,128)(2,1)}) fusion(f32[128]{0:T(128)S(1)} %get-tuple-element.286, f32[10,128]{1,0:T(8,128)S(1)} %broadcast_add_fusion.4, f32[128]{0:T(128)S(1)} %get-tuple-element.288, f32[10,128]{1,0:T(8,128)S(1)} %broadcast_add_fusion.5, f32[10]{0:T(128)S(1)} %compare_select_fusion.7), kind=kLoop, calls=%fused_computation.9.clone.1 | loop fusion | flops 2293760 | bytes 666664 | tf_op jit(solution)/shard_map/convert
  32.6 0.6 gather_fusion
  33.2 4.3 %fusion.40 = f32[10,512,2,128]{3,1,2,0:T(8,128)} fusion(bf16[10,128,512]{2,1,0:T(8,128)(2,1)S(1)} %gather_fusion, bf16[10,1,128,128]{3,2,1,0:T(8,128)(2,1)} %get-tuple-element.290, bf16[10,1,128,128]{3,2,1,0:T(8,128)(2,1)} %get-tuple-element.291), kind=kOutput, calls=%fused_computation.2.clone.1 | convolution fusion | flops 336855040 | bytes 7208960 | tf_op jit(solution)/shard_map/while/body/eval_jaxpr/pcij,pjm->picm/dot_general | solution.py:71
  37.5 2.8 %reduce_sum.18 = bf16[2,128,1024]{1,2,0:T(8,128)(2,1)S(1)} reduce(f32[2,5,128,1024]{2,3,1,0:T(8,128)} %bitcast.81, f32[]{:T(128)} %constant.246.clone.2..sunk), dimensions={1}, to_apply=%region_2.2 | reduce | flops 1048576 | bytes 5767172 | tf_op jit(solution)/shard_map/while/body/eval_jaxpr/reduce_sum | solution.py:96
  40.3 0.2 copy.32
  40.6 0.8 constant_dynamic-update-slice_fusion.2
  41.4 0.1 constant_dynamic-slice_fusion.2
  41.5 0.7 compare_select_fusion.7
  42.2 0.1 broadcast_add_fusion.4
  42.3 0.1 broadcast_add_fusion.5
  42.3 3.5 %fusion.39 = (bf16[10,1,128,128]{3,2,1,0:T(8,128)(2,1)}, bf16[10,1,128,128]{3,2,1,0:T(8,128)(2,1)}) fusion(f32[128]{0:T(128)S(1)} %get-tuple-element.286, f32[10,128]{1,0:T(8,128)S(1)} %broadcast_add_fusion.4, f32[128]{0:T(128)S(1)} %get-tuple-element.288, f32[10,128]{1,0:T(8,128)S(1)} %broadcast_add_fusion.5, f32[10]{0:T(128)S(1)} %compare_select_fusion.7), kind=kLoop, calls=%fused_computation.9.clone.1 | loop fusion | flops 2293760 | bytes 666664 | tf_op jit(solution)/shard_map/convert
  45.9 0.6 gather_fusion
  46.5 4.3 %fusion.40 = f32[10,512,2,128]{3,1,2,0:T(8,128)} fusion(bf16[10,128,512]{2,1,0:T(8,128)(2,1)S(1)} %gather_fusion, bf16[10,1,128,128]{3,2,1,0:T(8,128)(2,1)} %get-tuple-element.290, bf16[10,1,128,128]{3,2,1,0:T(8,128)(2,1)} %get-tuple-element.291), kind=kOutput, calls=%fused_computation.2.clone.1 | convolution fusion | flops 336855040 | bytes 7208960 | tf_op jit(solution)/shard_map/while/body/eval_jaxpr/pcij,pjm->picm/dot_general | solution.py:71
  50.8 2.8 %reduce_sum.18 = bf16[2,128,1024]{1,2,0:T(8,128)(2,1)S(1)} reduce(f32[2,5,128,1024]{2,3,1,0:T(8,128)} %bitcast.81, f32[]{:T(128)} %constant.246.clone.2..sunk), dimensions={1}, to_apply=%region_2.2 | reduce | flops 1048576 | bytes 5767172 | tf_op jit(solution)/shard_map/while/body/eval_jaxpr/reduce_sum | solution.py:96
  53.6 0.2 copy.32
  53.8 0.8 constant_dynamic-update-slice_fusion.2
  54.7 1.9 %fusion.26 = f32[512,1024]{1,0:T(8,128)S(1)} fusion(bf16[512,512]{1,0:T(8,128)(2,1)S(1)} %bitcast.83, bf16[512,1024]{1,0:T(8,128)(2,1)} %bitcast.84), kind=kOutput, calls=%fused_computation.62 | convolution fusion | flops 536870912 | bytes 3670016 | tf_op jit(solution)/shard_map/dot_general | solution.py:102
  56.6 1.5 %fusion.24 = (f32[512,512]{1,0:T(8,128)}, f32[512,512]{1,0:T(8,128)}) fusion(f32[512,1024]{1,0:T(8,128)S(1)} %fusion.26), kind=kLoop, calls=%fused_computation.60 | loop fusion | bytes 4194304 | tf_op jit(solution)/shard_map/slice | solution.py:105
  58.2 2.6 %copy.23 = f32[512,512]{0,1:T(8,128)} copy(f32[512,512]{1,0:T(8,128)} %get-tuple-element.240) | data formatting | bytes 2097152 | tf_op jit(solution)/shard_map/slice | solution.py:106
  60.8 2.6 %copy.30 = f32[512,512]{0,1:T(8,128)} copy(f32[512,512]{1,0:T(8,128)} %get-tuple-element.239) | data formatting | bytes 2097152
  63.3 2.0 %fusion.23 = (f32[1,512,512]{2,1,0:T(8,128)S(1)}, f32[1,512,512]{2,1,0:T(8,128)S(1)}) fusion(f32[512,512]{0,1:T(8,128)} %copy.30, f32[512,1024]{1,0:T(8,128)S(1)} %fusion.26, f32[512,512]{0,1:T(8,128)} %copy.23), kind=kLoop, calls=%fused_computation.53 | loop fusion | flops 524288 | bytes 6291456 | tf_op jit(solution)/shard_map/stack | solution.py:107
  65.4 1.5 pad_maximum_fusion
  66.9 0.0 reduce-scatter.3.cloned.1.call-update
  66.9 0.0 reduce-scatter.5.cloned.1.call-start
  66.9 68.5 %reduce-scatter.3.cloned.1.call-done = f32[2,32,512]{2,1,0:T(8,128)} async-done(((f32[2,512,512]{2,1,0:T(8,128)}), f32[2,32,512]{2,1,0:T(8,128)}) %reduce-scatter.3.cloned.1.call-update) | async-done | bytes 131088 | tf_op jit(solution)/shard_map/reduce_scatter | solution.py:108
  135.4 0.0 reduce-scatter.5.cloned.1.call-update
  135.4 11.5 %reduce-scatter.5.cloned.1.call-done = f32[2,32,256]{2,1,0:T(8,128)} async-done(((f32[2,32,512]{2,1,0:T(8,128)}), f32[2,32,256]{2,1,0:T(8,128)}) %reduce-scatter.5.cloned.1.call-update) | async-done | bytes 65552 | tf_op jit(solution)/shard_map/reduce_scatter | solution.py:109
  (14 shorter events, 0.1 us)
Async XLA Ops:
  6.5 4.5 %copy-start = (s32[1,1,3,20]{3,1,2,0:T(1,128)S(1)}, s32[1,1,3,20]{3,1,2,0:T(1,128)}, u32[]{:S(2)}) copy-start(s32[1,1,3,20]{3,1,2,0:T(1,128)} %param.8) | copy-start | bytes 724
  6.5 128.9 %reduce-scatter.3.cloned.1.call-start = ((), (), s32[]{:S(2)}) async-start(), calls=%async_computation.2 | async-start | bytes 2228224 | tf_op jit(solution)/shard_map/reduce_scatter | solution.py:108
  8.0 10.1 %collective-permute-start = (bf16[2,1,128,512]{3,2,1,0:T(8,128)(2,1)S(1)}, bf16[2,1,128,512]{3,2,1,0:T(8,128)(2,1)S(1)}, u32[]{:S(2)}, u32[]{:S(2)}) collective-permute-start(bf16[2,1,128,512]{3,2,1,0:T(8,128)(2,1)S(1)} %get-tuple-element.241), channel_id=1, source_target_pairs={{0,1},{1,0},{2,3},{3,2},{4,5},{5,4},{6,7},{7,6},{8,9},{9,8},{10,11... | collective-permute-start | bytes 786440 | tf_op jit(solution)/shard_map/ppermute | solution.py:21
  11.0 11.9 %collective-permute-start.1 = (bf16[2,1,128,512]{3,2,1,0:T(8,128)(2,1)S(1)}, bf16[2,1,128,512]{3,2,1,0:T(8,128)(2,1)S(1)}, u32[]{:S(2)}, u32[]{:S(2)}) collective-permute-start(bf16[2,1,128,512]{3,2,1,0:T(8,128)(2,1)S(1)} %get-tuple-element.242), channel_id=1, source_target_pairs={{1,0},{0,1},{3,2},{2,3},{5,4},{4,5},{7,6},{6,7},{9,8},{8,9},{11,10... | collective-permute-start | bytes 786440 | tf_op jit(solution)/shard_map/ppermute | solution.py:24
  23.0 3.8 %collective-permute-start.2 = (bf16[1,4,128,512]{3,2,1,0:T(8,128)(2,1)S(1)}, bf16[1,4,128,512]{3,2,1,0:T(8,128)(2,1)S(1)}, u32[]{:S(2)}, u32[]{:S(2)}) collective-permute-start(bf16[1,4,128,512]{3,2,1,0:T(8,128)(2,1)S(1)} %pad_maximum_fusion.2), channel_id=1, source_target_pairs={{2,0},{4,2},{6,4},{8,6},{10,8},{12,10},{14,12},{16,14},{18,16},{20... | collective-permute-start | bytes 1572872 | tf_op jit(solution)/shard_map/ppermute | solution.py:32
  66.9 80.1 %reduce-scatter.5.cloned.1.call-start = ((), (), s32[]{:S(2)}) async-start(), calls=%async_computation.3 | async-start | bytes 196608 | tf_op jit(solution)/shard_map/reduce_scatter | solution.py:109
Sparse Core Ops, SparseCore 0:
  67.0 68.3 reduce-scatter.2
  137.7 9.2 reduce-scatter.4
where the time goes:
time: 154 us
  waiting for transfers between devices  92 us (60%)
  other arithmetic  21.2 us (14%)
  between operations  13.5 us (9%)
  local copies, waits for them, and re-layouts  12.1 us (8%)
  matrix products  10.5 us (7%)
  starting transfers between devices  4.42 us (3%)
    reduce_scatter x1, waiting for transfers between devices, body(): lax.psum_scatter(summand, 'axial', scatter_dimension=1, tiled=True)  68.5 us
    reduce_scatter x1, waiting for transfers between devices, body(): lax.psum_scatter(partial_value, 'circ', scatter_dimension=2, tiled=True)  11.5 us
    dot_general x2, matrix products, slot_products(): jnp.einsum('pcij,pjm->picm', tiles, columns, preferred_element_type=jnp.f...  8.56 us
    another operation x2, other arithmetic  7.06 us
    ppermute x1, waiting for transfers between devices, with_halo(): lax.ppermute(lax.slice_in_dim(block, block.shape[dim] - width, None, axis...  6.96 us
    reduce_sum x2, other arithmetic, add_row(): jnp.sum(products.reshape(around_blocks, 5, patch_count, 2 * mode_count),...  5.59 us
    ppermute x1, waiting for transfers between devices, with_halo(): lax.ppermute(lax.slice_in_dim(block, 0, width, axis=dim), axis, backward)  4.79 us
    another operation x2, other arithmetic, body(): summand = jnp.stack([real_part + real_part.T, imag_part - imag_part.T])  3.54 us
  transfers between devices with their start and end apart: 5, of which 5 were waited for; matrix products, arithmetic and copies ran while one was open for 2% of the time, Pallas kernels for 0%

commit v1 on v0

v1 whole, which is shorter than its diff:
```python
import functools

import numpy as np
import ml_dtypes
import jax
import jax.numpy as jnp
from jax import lax
from jax.experimental import pallas as pl
from jax.experimental.pallas import tpu as pltpu
from jax.sharding import PartitionSpec as P

ALONG = 16
AROUND = 8
PATCH = ALONG * AROUND
DECAY_A = 0.125
DECAY_C = 0.16
WAVE = 0.6
KINDS = ((0, 0), (0, 1), (1, -1), (1, 0), (1, 1))
HALO = 112
HALO_PAD = 128
MESH = pl.DeviceIdType.MESH


def split(values):
    high = values.astype(ml_dtypes.bfloat16)
    low = (values - high.astype(np.float64)).astype(ml_dtypes.bfloat16)
    return high, low


@functools.lru_cache(None)
def tables():
    index = np.arange(PATCH)
    along, around = index // AROUND, index % AROUND
    tiles = []
    for step_a, step_c in KINDS:
        gap_a = (step_a * ALONG + along[None, :] - along[:, None]).astype(np.float32)
        gap_c = (step_c * AROUND + around[None, :] - around[:, None]).astype(np.float32)
        weight = np.float32(0.5 if (step_a, step_c) == (0, 0) else 1.0)
        envelope = weight * np.exp(np.float32(-DECAY_A) * np.abs(gap_a) - np.float32(DECAY_C) * np.abs(gap_c))
        angle = np.float32(WAVE) * gap_a
        tiles.append(np.concatenate([envelope * np.cos(angle), -envelope * np.sin(angle)]))
    tiles = np.stack(tiles).astype(ml_dtypes.bfloat16)

    g = np.zeros((40, PATCH))
    forward = np.exp(-DECAY_C * around)
    backward = np.exp(-DECAY_C * (AROUND - around))
    phase = np.exp((-DECAY_A - 1j * WAVE) * along)
    for k in range(ALONG):
        g[k] = forward * (along == k)
    for k in range(AROUND):
        g[16 + k] = phase.real * (around == k)
        g[24 + k] = phase.imag * (around == k)
    g[32], g[33] = (phase * forward).real, (phase * forward).imag
    g[34], g[35] = (phase * backward).real, (phase * backward).imag
    gather = np.concatenate(split(g))

    spread = np.zeros((4, PATCH, HALO_PAD), np.complex128)
    code = np.full((HALO_PAD, 1), -1, np.int32)
    alpha = np.exp((-DECAY_A - 1j * WAVE) * (ALONG - along))
    ahead = np.exp(-DECAY_C * (AROUND - around))
    behind = np.exp(-DECAY_C * around)

    def around_sums(block, base):
        for k in range(ALONG):
            gap = k - along
            spread[block, :, base + k] = np.exp(-DECAY_A * np.abs(gap) - 1j * WAVE * gap) * ahead
            code[base + k] = block * 5 + 1

    def along_sums(block, base):
        for k in range(AROUND):
            value = alpha * np.exp(-DECAY_C * np.abs(k - around))
            spread[block, :, base + k] = value
            spread[block, :, base + 8 + k] = 1j * value
            code[base + k] = code[base + 8 + k] = block * 5 + 3

    def both_sums(block, base, kind):
        value = alpha * (ahead if kind == 4 else behind)
        spread[block, :, base] = value
        spread[block, :, base + 1] = 1j * value
        code[base] = code[base + 1] = block * 5 + kind

    around_sums(1, 0)
    around_sums(3, 16)
    both_sums(1, 32, 4)
    both_sums(0, 40 + 2, 2)
    along_sums(2, 48)
    both_sums(3, 48 + 18, 2)
    along_sums(3, 72)
    both_sums(2, 72 + 16, 4)
    both_sums(3, 96, 4)
    both_sums(2, 104 + 2, 2)
    spread = spread.reshape(4 * PATCH, HALO_PAD)
    spread = np.stack(split(np.concatenate([spread.real, spread.imag], axis=1)))
    return tiles, gather, spread, code


LOCAL = ((0, 1, 3, 4), (0, 2, 3), (0, 1), (0,))
MESSAGES = ((0, -1, 0, 40), (0, 1, 40, 8), (-1, 0, 48, 48), (-1, -1, 96, 8), (-1, 1, 104, 8))


def parts(value):
    high = value.astype(jnp.bfloat16)
    return high, (value - high.astype(jnp.float32)).astype(jnp.bfloat16)


def dot(a, b):
    return jnp.dot(a, b, preferred_element_type=jnp.float32)


def spectrum(axial, circ, shapes_ref, amp_ref, list_ref, count_ref, tiles_ref, gather_ref, spread_ref, code_ref,
             halo_out, halo_in, halo_send, halo_recv, weighted, relations):
    a, c = lax.axis_index("axial"), lax.axis_index("circ")
    modes = shapes_ref.shape[-1]

    def device(step_a, step_c):
        return (lax.rem(a + step_a + axial, axial), lax.rem(c + step_c + circ, circ))

    halo_in[...] = jnp.zeros_like(halo_in)
    barrier = pltpu.get_barrier_semaphore()
    greeted = [device(sa, sc) for sa, sc, _, _ in MESSAGES] + [device(-sa, -sc) for sa, sc, _, _ in MESSAGES] + relations
    for target in greeted:
        pl.semaphore_signal(barrier, inc=1, device_id=target, device_id_type=MESH)

    sums = []
    for block in range(4):
        i, j = block // 2, block % 2
        column = jnp.broadcast_to(amp_ref[i, j : j + 1, :], (PATCH, PATCH)).T
        wide = jnp.concatenate([column] * (modes // PATCH), axis=1)
        weighted[block * PATCH : (block + 1) * PATCH, :] = (shapes_ref[i, j] * wide).astype(jnp.bfloat16)
        both = dot(gather_ref[...], weighted[block * PATCH : (block + 1) * PATCH, :])
        sums.append(both[:40] + both[40:])
    halo_out[0:16] = sums[0][0:16]
    halo_out[16:32] = sums[2][0:16]
    halo_out[32:40] = sums[2][32:40]
    halo_out[40:48] = sums[3][32:40]
    halo_out[48:72] = sums[0][16:40]
    halo_out[72:96] = sums[1][16:40]
    halo_out[96:104] = sums[0][32:40]
    halo_out[104:112] = sums[1][32:40]
    pl.semaphore_wait(barrier, len(greeted))

    def copy_of(at):
        step_a, step_c, base, rows = MESSAGES[at]
        return pltpu.make_async_remote_copy(
            src_ref=halo_out.at[pl.ds(base, rows)],
            dst_ref=halo_in.at[pl.ds(base, rows)],
            send_sem=halo_send.at[at],
            recv_sem=halo_recv.at[at],
            device_id=device(step_a, step_c),
            device_id_type=MESH,
        )

    for at in range(2):
        copy_of(at).start()

    @pl.when(a > 0)
    def _():
        for at in range(2, 5):
            copy_of(at).start()

    listing = list_ref[0, 0]
    slot_code = listing[0:1] * 5 + listing[1:2] * 3 + listing[2:3]
    kept = lax.broadcasted_iota(jnp.int32, slot_code.shape, 1) < count_ref[...]
    slot_code = jnp.where(kept, slot_code, -2)
    wanted = lax.broadcasted_iota(jnp.int32, (24, slot_code.shape[1]), 0)
    weights = jnp.sum(jnp.where(wanted == slot_code, 1.0, 0.0), axis=1, keepdims=True)
    halo_weights = jnp.sum(jnp.where(code_ref[...] == slot_code, 1.0, 0.0), axis=1, keepdims=True)

    real_sums, imag_sums = [], []
    for block in range(4):
        tiles = []
        for kind in LOCAL[block]:
            at = block * 5 + kind
            tiles.append(tiles_ref[kind] * jnp.broadcast_to(weights[at : at + 1], (2 * PATCH, PATCH)).astype(jnp.bfloat16))
        tile = tiles[0] if len(tiles) == 1 else jnp.concatenate(tiles, axis=1)
        total = dot(tile, weighted[(4 - len(tiles)) * PATCH :, :])
        real_sums.append(total[:PATCH])
        imag_sums.append(total[PATCH:])
    turned = weighted[...].T
    real_high, real_low = parts(jnp.concatenate(real_sums, axis=0))
    imag_high, imag_low = parts(jnp.concatenate(imag_sums, axis=0))
    real_cross = dot(turned, real_high) + dot(turned, real_low)
    imag_cross = dot(turned, imag_high) + dot(turned, imag_low)
    through = dot(turned, spread_ref[0]) + dot(turned, spread_ref[1])
    high, low = parts(through)
    real_left = jnp.concatenate([x[:, :HALO_PAD] for x in (high, low, high)], axis=1)
    imag_left = jnp.concatenate([x[:, HALO_PAD:] for x in (high, low, high)], axis=1)

    for at in range(2):
        copy_of(at).wait_recv()

    @pl.when(a < axial - 1)
    def _():
        for at in range(2, 5):
            copy_of(at).wait_recv()

    received_high, received_low = parts(halo_in[...] * halo_weights)
    right = jnp.concatenate([received_high, received_high, received_low], axis=0)
    real_cross = real_cross + dot(real_left, right)
    imag_cross = imag_cross + dot(imag_left, right)

    for at in range(2):
        copy_of(at).wait_send()

    @pl.when(a > 0)
    def _():
        for at in range(2, 5):
            copy_of(at).wait_send()

    return real_cross + real_cross.T, imag_cross - imag_cross.T


def plain_kernel(axial, circ, shapes_ref, amp_ref, list_ref, count_ref, tiles_ref, gather_ref, spread_ref, code_ref, out_ref,
                 halo_out, halo_in, halo_send, halo_recv, weighted):
    real, imag = spectrum(axial, circ, shapes_ref, amp_ref, list_ref, count_ref, tiles_ref, gather_ref, spread_ref, code_ref,
                          halo_out, halo_in, halo_send, halo_recv, weighted, [])
    out_ref[0] = real
    out_ref[1] = imag


def full_kernel(axial, circ, shapes_ref, amp_ref, list_ref, count_ref, tiles_ref, gather_ref, spread_ref, code_ref, out_ref,
                halo_out, halo_in, halo_send, halo_recv, weighted,
                pieces, recv0, recv1, recv2, recv3, send_sem, recv_sem):
    a, c = lax.axis_index("axial"), lax.axis_index("circ")
    depth = axial // 4
    core, y, z = lax.rem(a, 2), lax.rem(a // 2, 2), a // 4
    flip_core = (a + 1 - 2 * core, c)
    first_a = a + core * (2 - 4 * y)
    first_c = c + (1 - core) * (1 - 2 * c)
    second_a = a + (1 - core) * (2 - 4 * y)
    second_c = c + core * (1 - 2 * c)
    key1 = core * y + (1 - core) * c
    key2 = core * c + (1 - core) * y
    slices = [(lax.rem(z + d, depth) * 4 + lax.rem(a, 4), c) for d in range(1, depth)]
    relations = [flip_core, (first_a, first_c), (second_a, second_c)] + slices

    real, imag = spectrum(axial, circ, shapes_ref, amp_ref, list_ref, count_ref, tiles_ref, gather_ref, spread_ref, code_ref,
                          halo_out, halo_in, halo_send, halo_recv, weighted, relations)
    rows, columns = real.shape[0] // axial, real.shape[1] // circ
    for to_core in range(2):
        for to_y in range(2):
            for to_x in range(2):
                for to_z in range(depth):
                    start = (to_z * 4 + to_y * 2 + to_core) * rows
                    place = (to_core,) + ((to_x, to_y) if to_core == 0 else (to_y, to_x)) + (to_z,)
                    for part, value in enumerate((real, imag)):
                        pieces[place + (part,)] = value[start : start + rows, to_x * columns : (to_x + 1) * columns]

    def send(source, target, at, device):
        copy = pltpu.make_async_remote_copy(
            src_ref=source, dst_ref=target, send_sem=send_sem.at[at], recv_sem=recv_sem.at[at], device_id=device, device_id_type=MESH
        )
        copy.start()
        return copy

    copies = [send(pieces.at[1 - core], recv0, 0, flip_core)]
    copies[0].wait_recv()
    recv0[1 - key1] = recv0[1 - key1] + pieces[core, 1 - key1]
    copies.append(send(recv0.at[1 - key1], recv1, 1, (first_a, first_c)))
    own = recv0[key1] + pieces[core, key1]
    recv0[key1] = own
    copies[1].wait_recv()
    recv1[1 - key2] = recv1[1 - key2] + recv0[key1, 1 - key2]
    copies.append(send(recv1.at[1 - key2], recv2, 2, (second_a, second_c)))
    recv1[key2] = recv1[key2] + recv0[key1, key2]
    copies[2].wait_recv()
    recv2[...] = recv2[...] + recv1[key2]
    for d in range(1, depth):
        copies.append(send(recv2.at[lax.rem(z + d, depth)], recv3.at[d - 1], 2 + d, slices[d - 1]))
    total = recv2[z]
    for d in range(1, depth):
        copies[2 + d].wait_recv()
        total = total + recv3[d - 1]
    out_ref[...] = total
    for copy in copies:
        copy.wait_send()


def solution(mesh):
    axial, circ = mesh.shape["axial"], mesh.shape["circ"]

    def body(mode_shapes, amplitude, pair_list, pair_counts):
        modes = mode_shapes.shape[-1]
        constants = tables()
        rows, columns = modes // axial, modes // circ
        vmem = pl.BlockSpec(memory_space=pltpu.VMEM)
        scratch = [
            pltpu.VMEM((HALO, modes), jnp.float32),
            pltpu.VMEM((HALO_PAD, modes), jnp.float32),
            pltpu.SemaphoreType.DMA((5,)),
            pltpu.SemaphoreType.DMA((5,)),
            pltpu.VMEM((4 * PATCH, modes), jnp.bfloat16),
        ]
        together = circ == 2 and axial % 4 == 0 and rows % 8 == 0 and columns % 128 == 0
        depth = axial // 4
        if together:
            kernel, shape = full_kernel, (2, rows, columns)
            piece = (depth, 2, rows, columns)
            scratch += [
                pltpu.VMEM((2, 2, 2) + piece, jnp.float32),
                pltpu.VMEM((2, 2) + piece, jnp.float32),
                pltpu.VMEM((2,) + piece, jnp.float32),
                pltpu.VMEM(piece, jnp.float32),
                pltpu.VMEM((depth - 1,) + piece[1:], jnp.float32),
                pltpu.SemaphoreType.DMA((2 + depth,)),
                pltpu.SemaphoreType.DMA((2 + depth,)),
            ]
        else:
            kernel, shape = plain_kernel, (2, modes, modes)
        result = pl.pallas_call(
            functools.partial(kernel, axial, circ),
            out_shape=jax.ShapeDtypeStruct(shape, jnp.float32),
            in_specs=[vmem] * 8,
            out_specs=vmem,
            scratch_shapes=scratch,
            compiler_params=pltpu.CompilerParams(collective_id=0, has_side_effects=True, vmem_limit_bytes=40 * 1024 * 1024),
        )(mode_shapes, amplitude, pair_list, pair_counts, *constants)
        if not together:
            result = lax.psum_scatter(result, "axial", scatter_dimension=1, tiled=True)
            result = lax.psum_scatter(result, "circ", scatter_dimension=2, tiled=True)
        return result

    in_specs = (
        P("axial", "circ", None, None),
        P("axial", "circ", None),
        P("axial", "circ", None, None),
        P("axial", "circ"),
    )
    return jax.shard_map(body, mesh=mesh, in_specs=in_specs, out_specs=P(None, "axial", "circ"), check_vma=False)
```

time: 154 us -> 40.7 us (0.26)
  waiting for transfers between devices: 92 us -> 0 us
  Pallas kernels: 0 us -> 33.5 us
  other arithmetic: 21.2 us -> 0 us
  between operations: 13.5 us -> 0.69 us
  matrix products: 10.5 us -> 0 us
  local copies, waits for them, and re-layouts: 12.1 us -> 6.12 us
  starting transfers between devices: 4.42 us -> 0 us
    reduce_scatter x2 -> x0, waiting for transfers between devices: 80 us -> none  [the longest x1 68.5 us: body(): lax.psum_scatter(summand, 'axial', scatter_dimension=1, tiled=True)]
    pallas_call x0 -> x1, Pallas kernels: none -> 33.5 us  [body(): pl.pallas_call(functools.partial(kernel, axial, circ), out_shape=jax.Shap...]
    ppermute x3 -> x0, waiting for transfers between devices: 11.9 us -> none  [the longest x1 6.96 us: with_halo(): lax.ppermute(lax.slice_in_dim(block, block.shape[dim] - width, None, axis...]
    another operation x4 -> x0, other arithmetic: 10.6 us -> none
    dot_general x3 -> x0, matrix products: 10.5 us -> none  [the longest x2 8.56 us: slot_products(): jnp.einsum('pcij,pjm->picm', tiles, columns, preferred_element_type=jnp.f...]
    reduce_sum x2 -> x0, other arithmetic: 5.59 us -> none  [add_row(): jnp.sum(products.reshape(around_blocks, 5, patch_count, 2 * mode_count),...]
    ppermute x3 -> x0, starting transfers between devices: 4.37 us -> none  [the longest x1 3 us: with_halo(): lax.ppermute(lax.slice_in_dim(block, block.shape[dim] - width, None, axis...]
    slice x3 -> x0, local copies, waits for them, and re-layouts: 4.17 us -> none  [the longest x1 2.59 us: body(): imag_part = cross[:, mode_count:]]
  transfers between devices with their start and end apart: 5 -> 0, of which waited for: 5 -> 0; matrix products, arithmetic and copies ran while one was open for 2% -> 0% of each run, Pallas kernels for 0% -> 0%
where the time goes in v1:
time: 40.7 us; the launch traced here: 40.3 us
  Pallas kernels  33.5 us (82%)
  local copies, waits for them, and re-layouts  6.12 us (15%)
  between operations  0.69 us (2%)
    pallas_call x1, Pallas kernels, body(): pl.pallas_call(functools.partial(kernel, axial, circ), out_shape=jax.Shap...  33.5 us
    unnamed x16, local copies, waits for them, and re-layouts  6.12 us

profile of v1, /device:TPU:0, one launch (start us, length us, event | category | flops | bytes accessed | tf_op | source)
XLA Modules:
  0.0 40.3 jit_solution(16348511039871523629)
XLA Ops:
  0.0 0.0 copy-start.6
  0.7 0.0 copy-done.6
  0.7 0.0 copy-start.5
  0.7 0.7 %copy-done.5 = f32[2,2,128]{2,1,0:T(2,128)S(1)} copy-done((f32[2,2,128]{2,1,0:T(2,128)S(1)}, f32[2,2,128]{2,1,0:T(2,128)}, u32[]{:S(2)}) %copy-start.5) | copy-done | bytes 2072
  1.4 0.0 copy-start
  1.4 1.2 %copy-done = f32[2,2,128,512]{3,2,1,0:T(8,128)S(1)} copy-done((f32[2,2,128,512]{3,2,1,0:T(8,128)S(1)}, f32[2,2,128,512]{3,2,1,0:T(8,128)}, u32[]{:S(2)}) %copy-start) | copy-done | bytes 1048600
  2.6 0.0 copy-start.1
  2.6 1.0 %copy-done.1 = bf16[2,512,256]{2,1,0:T(8,128)(2,1)S(1)} copy-done((bf16[2,512,256]{2,1,0:T(8,128)(2,1)S(1)}, bf16[2,512,256]{2,1,0:T(8,128)(2,1)}, u32[]{:S(2)}) %copy-start.1) | copy-done | bytes 524312
  3.6 0.0 copy-start.2
  3.6 1.0 %copy-done.2 = bf16[5,256,128]{2,1,0:T(8,128)(2,1)S(1)} copy-done((bf16[5,256,128]{2,1,0:T(8,128)(2,1)S(1)}, bf16[5,256,128]{2,1,0:T(8,128)(2,1)}, u32[]{:S(2)}) %copy-start.2) | copy-done | bytes 327704
  4.6 0.0 copy-start.3
  4.6 0.8 %copy-done.3 = s32[128,1]{1,0:T(8,128)S(1)} copy-done((s32[128,1]{1,0:T(8,128)S(1)}, s32[128,1]{1,0:T(8,128)}, u32[]{:S(2)}) %copy-start.3) | copy-done | bytes 536
  5.4 0.0 copy-start.4
  5.4 0.7 %copy-done.4 = bf16[80,128]{1,0:T(8,128)(2,1)S(1)} copy-done((bf16[80,128]{1,0:T(8,128)(2,1)S(1)}, bf16[80,128]{1,0:T(8,128)(2,1)}, u32[]{:S(2)}) %copy-start.4) | copy-done | bytes 20504
  6.2 33.5 %shard_map.82 = f32[2,32,256]{2,1,0:T(8,128)S(1)} custom-call(f32[2,2,128,512]{3,2,1,0:T(8,128)S(1)} %copy-done, f32[2,2,128]{2,1,0:T(2,128)S(1)} %copy-done.5, s32[1,1,3,20]{3,2,1,0:T(4,128)S(1)} %copy.9.list_ref, s32[1,1]{1,0:T(1,128)S(6)} %copy.11.count_ref, bf16[5,256,128]{2,1,0:T(8,128)(2,1)S(1)} %copy-done.2, bf16[80,128]{1,0:T(8,128)(2,1)S(1)} %copy-done.4, ...), custom_call_target="tpu_custom_call" | custom-call | tf_op jit(solution)/shard_map/pallas_call | solution.py:310
  39.7 0.6 %copy.12 = f32[2,32,256]{2,1,0:T(8,128)} copy(f32[2,32,256]{2,1,0:T(8,128)S(1)} %shard_map.82) | data formatting | bytes 131072
  (1 shorter events, 0.0 us)
Async XLA Ops:
  0.0 0.7 %copy-start.6 = (s32[1,1,3,20]{3,1,2,0:T(1,128)S(1)}, s32[1,1,3,20]{3,1,2,0:T(1,128)}, u32[]{:S(2)}) copy-start(s32[1,1,3,20]{3,1,2,0:T(1,128)} %param.10) | copy-start | bytes 724
  0.7 0.7 %copy-start.5 = (f32[2,2,128]{2,1,0:T(2,128)S(1)}, f32[2,2,128]{2,1,0:T(2,128)}, u32[]{:S(2)}) copy-start(f32[2,2,128]{2,1,0:T(2,128)} %amp_ref.1) | copy-start | bytes 6148
  1.4 1.2 %copy-start = (f32[2,2,128,512]{3,2,1,0:T(8,128)S(1)}, f32[2,2,128,512]{3,2,1,0:T(8,128)}, u32[]{:S(2)}) copy-start(f32[2,2,128,512]{3,2,1,0:T(8,128)} %shapes_ref.1) | copy-start | bytes 3145732
  2.6 1.0 %copy-start.1 = (bf16[2,512,256]{2,1,0:T(8,128)(2,1)S(1)}, bf16[2,512,256]{2,1,0:T(8,128)(2,1)}, u32[]{:S(2)}) copy-start(bf16[2,512,256]{2,1,0:T(8,128)(2,1)} %constant.10.clone.spread_ref) | copy-start | bytes 1572868
  3.6 1.0 %copy-start.2 = (bf16[5,256,128]{2,1,0:T(8,128)(2,1)S(1)}, bf16[5,256,128]{2,1,0:T(8,128)(2,1)}, u32[]{:S(2)}) copy-start(bf16[5,256,128]{2,1,0:T(8,128)(2,1)} %constant.8.clone.tiles_ref) | copy-start | bytes 983044
  4.6 0.8 %copy-start.3 = (s32[128,1]{1,0:T(8,128)S(1)}, s32[128,1]{1,0:T(8,128)}, u32[]{:S(2)}) copy-start(s32[128,1]{1,0:T(8,128)} %constant.11.clone.code_ref) | copy-start | bytes 1540
  5.4 0.7 %copy-start.4 = (bf16[80,128]{1,0:T(8,128)(2,1)S(1)}, bf16[80,128]{1,0:T(8,128)(2,1)}, u32[]{:S(2)}) copy-start(bf16[80,128]{1,0:T(8,128)(2,1)} %constant.9.clone.gather_ref) | copy-start | bytes 61444

commit v2 on v1

--- a/solution.py
+++ b/solution.py
@@ -18,6 +18,7 @@
 KINDS = ((0, 0), (0, 1), (1, -1), (1, 0), (1, 1))
 HALO = 112
 HALO_PAD = 128
+LIMIT = 32767.0
 MESH = pl.DeviceIdType.MESH
 
 
@@ -107,10 +108,21 @@
     return jnp.dot(a, b, preferred_element_type=jnp.float32)
 
 
-def spectrum(axial, circ, shapes_ref, amp_ref, list_ref, count_ref, tiles_ref, gather_ref, spread_ref, code_ref,
-             halo_out, halo_in, halo_send, halo_recv, weighted, relations):
+def spectrum(axial, circ, operands, scratch, relations, deliver):
+    shapes_hbm, amp_ref, list_ref, count_ref, tiles_hbm, gather_hbm, spread_hbm, code_ref = operands
+    halo_out, halo_in, halo_send, halo_recv, weighted, shapes_ref, tiles_ref, gather_ref, spread_ref, fetch_sem = scratch
+    fetches = [
+        pltpu.make_async_copy(source, target, fetch_sem.at[at])
+        for at, (source, target) in enumerate(
+            [(gather_hbm, gather_ref)]
+            + [(shapes_hbm.at[block // 2, block % 2], shapes_ref.at[block // 2, block % 2]) for block in range(4)]
+            + [(tiles_hbm, tiles_ref), (spread_hbm, spread_ref)]
+        )
+    ]
+    for fetch in fetches:
+        fetch.start()
     a, c = lax.axis_index("axial"), lax.axis_index("circ")
-    modes = shapes_ref.shape[-1]
+    modes = weighted.shape[-1]
 
     def device(step_a, step_c):
         return (lax.rem(a + step_a + axial, axial), lax.rem(c + step_c + circ, circ))
@@ -122,7 +134,9 @@
         pl.semaphore_signal(barrier, inc=1, device_id=target, device_id_type=MESH)
 
     sums = []
+    fetches[0].wait()
     for block in range(4):
+        fetches[1 + block].wait()
         i, j = block // 2, block % 2
         column = jnp.broadcast_to(amp_ref[i, j : j + 1, :], (PATCH, PATCH)).T
         wide = jnp.concatenate([column] * (modes // PATCH), axis=1)
@@ -158,14 +172,14 @@
         for at in range(2, 5):
             copy_of(at).start()
 
-    listing = list_ref[0, 0]
-    slot_code = listing[0:1] * 5 + listing[1:2] * 3 + listing[2:3]
+    slot_code = list_ref[0] * 5 + list_ref[1] * 3 + list_ref[2]
     kept = lax.broadcasted_iota(jnp.int32, slot_code.shape, 1) < count_ref[...]
     slot_code = jnp.where(kept, slot_code, -2)
     wanted = lax.broadcasted_iota(jnp.int32, (24, slot_code.shape[1]), 0)
     weights = jnp.sum(jnp.where(wanted == slot_code, 1.0, 0.0), axis=1, keepdims=True)
     halo_weights = jnp.sum(jnp.where(code_ref[...] == slot_code, 1.0, 0.0), axis=1, keepdims=True)
 
+    fetches[5].wait()
     real_sums, imag_sums = [], []
     for block in range(4):
         tiles = []
@@ -181,6 +195,7 @@
     imag_high, imag_low = parts(jnp.concatenate(imag_sums, axis=0))
     real_cross = dot(turned, real_high) + dot(turned, real_low)
     imag_cross = dot(turned, imag_high) + dot(turned, imag_low)
+    fetches[6].wait()
     through = dot(turned, spread_ref[0]) + dot(turned, spread_ref[1])
     high, low = parts(through)
     real_left = jnp.concatenate([x[:, :HALO_PAD] for x in (high, low, high)], axis=1)
@@ -197,7 +212,9 @@
     received_high, received_low = parts(halo_in[...] * halo_weights)
     right = jnp.concatenate([received_high, received_high, received_low], axis=0)
     real_cross = real_cross + dot(real_left, right)
+    deliver(0, real_cross + real_cross.T)
     imag_cross = imag_cross + dot(imag_left, right)
+    deliver(1, imag_cross - imag_cross.T)
 
     for at in range(2):
         copy_of(at).wait_send()
@@ -207,72 +224,116 @@
         for at in range(2, 5):
             copy_of(at).wait_send()
 
-    return real_cross + real_cross.T, imag_cross - imag_cross.T
-
-
-def plain_kernel(axial, circ, shapes_ref, amp_ref, list_ref, count_ref, tiles_ref, gather_ref, spread_ref, code_ref, out_ref,
-                 halo_out, halo_in, halo_send, halo_recv, weighted):
-    real, imag = spectrum(axial, circ, shapes_ref, amp_ref, list_ref, count_ref, tiles_ref, gather_ref, spread_ref, code_ref,
-                          halo_out, halo_in, halo_send, halo_recv, weighted, [])
-    out_ref[0] = real
-    out_ref[1] = imag
-
-
-def full_kernel(axial, circ, shapes_ref, amp_ref, list_ref, count_ref, tiles_ref, gather_ref, spread_ref, code_ref, out_ref,
-                halo_out, halo_in, halo_send, halo_recv, weighted,
-                pieces, recv0, recv1, recv2, recv3, send_sem, recv_sem):
+
+def plain_kernel(axial, circ, *refs):
+    out_ref = refs[8]
+
+    def deliver(part, value):
+        out_ref[part] = value
+
+    spectrum(axial, circ, refs[:8], refs[9:], [], deliver)
+
+
+def coded(read, write, count):
+    most = None
+    for at in range(count):
+        value = jnp.max(jnp.abs(read(at)), axis=0, keepdims=True)
+        most = value if most is None else jnp.maximum(most, value)
+    most = jnp.maximum(most, 1e-30)
+    factor = LIMIT / most
+    for at in range(count):
+        write(at, jnp.round(read(at) * factor).astype(jnp.int32).astype(jnp.int16))
+    return jnp.broadcast_to(most * (1.0 / LIMIT), (8, most.shape[1]))
+
+
+def decoded(value, scales):
+    return value.astype(jnp.int32).astype(jnp.float32) * scales[0:1]
+
+
+def full_kernel(axial, circ, *refs):
+    operands, out_ref, scratch = refs[:8], refs[8], refs[9:19]
+    pieces, sent, came, sent_scale, came_scale, send_sem, recv_sem = refs[19:]
     a, c = lax.axis_index("axial"), lax.axis_index("circ")
     depth = axial // 4
     core, y, z = lax.rem(a, 2), lax.rem(a // 2, 2), a // 4
     flip_core = (a + 1 - 2 * core, c)
-    first_a = a + core * (2 - 4 * y)
-    first_c = c + (1 - core) * (1 - 2 * c)
-    second_a = a + (1 - core) * (2 - 4 * y)
-    second_c = c + core * (1 - 2 * c)
+    first = (a + core * (2 - 4 * y), c + (1 - core) * (1 - 2 * c))
+    second = (a + (1 - core) * (2 - 4 * y), c + core * (1 - 2 * c))
     key1 = core * y + (1 - core) * c
     key2 = core * c + (1 - core) * y
     slices = [(lax.rem(z + d, depth) * 4 + lax.rem(a, 4), c) for d in range(1, depth)]
-    relations = [flip_core, (first_a, first_c), (second_a, second_c)] + slices
-
-    real, imag = spectrum(axial, circ, shapes_ref, amp_ref, list_ref, count_ref, tiles_ref, gather_ref, spread_ref, code_ref,
-                          halo_out, halo_in, halo_send, halo_recv, weighted, relations)
-    rows, columns = real.shape[0] // axial, real.shape[1] // circ
-    for to_core in range(2):
-        for to_y in range(2):
-            for to_x in range(2):
-                for to_z in range(depth):
-                    start = (to_z * 4 + to_y * 2 + to_core) * rows
-                    place = (to_core,) + ((to_x, to_y) if to_core == 0 else (to_y, to_x)) + (to_z,)
-                    for part, value in enumerate((real, imag)):
-                        pieces[place + (part,)] = value[start : start + rows, to_x * columns : (to_x + 1) * columns]
-
-    def send(source, target, at, device):
-        copy = pltpu.make_async_remote_copy(
-            src_ref=source, dst_ref=target, send_sem=send_sem.at[at], recv_sem=recv_sem.at[at], device_id=device, device_id_type=MESH
-        )
-        copy.start()
-        return copy
-
-    copies = [send(pieces.at[1 - core], recv0, 0, flip_core)]
-    copies[0].wait_recv()
-    recv0[1 - key1] = recv0[1 - key1] + pieces[core, 1 - key1]
-    copies.append(send(recv0.at[1 - key1], recv1, 1, (first_a, first_c)))
-    own = recv0[key1] + pieces[core, key1]
-    recv0[key1] = own
-    copies[1].wait_recv()
-    recv1[1 - key2] = recv1[1 - key2] + recv0[key1, 1 - key2]
-    copies.append(send(recv1.at[1 - key2], recv2, 2, (second_a, second_c)))
-    recv1[key2] = recv1[key2] + recv0[key1, key2]
-    copies[2].wait_recv()
-    recv2[...] = recv2[...] + recv1[key2]
-    for d in range(1, depth):
-        copies.append(send(recv2.at[lax.rem(z + d, depth)], recv3.at[d - 1], 2 + d, slices[d - 1]))
-    total = recv2[z]
-    for d in range(1, depth):
-        copies[2 + d].wait_recv()
-        total = total + recv3[d - 1]
-    out_ref[...] = total
-    for copy in copies:
+    rows, columns = out_ref.shape[1:]
+    base = (0, 4 * depth, 6 * depth) + tuple(7 * depth + d for d in range(depth - 1))
+    copies = {}
+
+    def send(part, step, read, count, device):
+        def write(at, value):
+            sent[part, base[step] + at] = value
+
+        sent_scale[part, step] = coded(read, write, count)
+        span = pl.ds(base[step], count)
+        for at, (source, target) in enumerate(
+            ((sent.at[part, span], came.at[part, span]), (sent_scale.at[part, step], came_scale.at[part, step]))
+        ):
+            copy = pltpu.make_async_remote_copy(
+                src_ref=source,
+                dst_ref=target,
+                send_sem=send_sem.at[part, step, at],
+                recv_sem=recv_sem.at[part, step, at],
+                device_id=device,
+                device_id_type=MESH,
+            )
+            copy.start()
+            copies[part, step, at] = copy
+
+    def receive(part, step):
+        for at in range(2):
+            copies[part, step, at].wait_recv()
+        return came_scale[part, step]
+
+    def deliver(part, value):
+        for to_core in range(2):
+            for to_y in range(2):
+                for to_x in range(2):
+                    for to_z in range(depth):
+                        start = (to_z * 4 + to_y * 2 + to_core) * rows
+                        place = (to_core,) + ((to_x, to_y) if to_core == 0 else (to_y, to_x))
+                        at = ((place[0] * 2 + place[1]) * 2 + place[2]) * depth + to_z
+                        pieces[part, at] = value[start : start + rows, to_x * columns : (to_x + 1) * columns]
+        other = (1 - core) * 4 * depth
+        send(part, 0, lambda at: pieces[part, other + at], 4 * depth, flip_core)
+
+    spectrum(axial, circ, operands, scratch, [flip_core, first, second] + slices, deliver)
+
+    def add(part, step, scales, own, offset, count):
+        for at in range(count):
+            pieces[part, own + offset + at] += decoded(came[part, base[step] + offset + at], scales)
+
+    for part in range(2):
+        scales = receive(part, 0)
+        own, give, keep = core * 4 * depth, (1 - key1) * 2 * depth, key1 * 2 * depth
+        add(part, 0, scales, own, give, 2 * depth)
+        send(part, 1, lambda at: pieces[part, own + give + at], 2 * depth, first)
+        add(part, 0, scales, own, keep, 2 * depth)
+    for part in range(2):
+        scales = receive(part, 1)
+        own, give, keep = core * 4 * depth + key1 * 2 * depth, (1 - key2) * depth, key2 * depth
+        add(part, 1, scales, own, give, depth)
+        send(part, 2, lambda at: pieces[part, own + give + at], depth, second)
+        add(part, 1, scales, own, keep, depth)
+    for part in range(2):
+        scales = receive(part, 2)
+        own = core * 4 * depth + key1 * 2 * depth + key2 * depth
+        add(part, 2, scales, own, 0, depth)
+        for d in range(1, depth):
+            send(part, 2 + d, lambda at: pieces[part, own + lax.rem(z + d, depth)], 1, slices[d - 1])
+    for part in range(2):
+        total = pieces[part, own + z]
+        for d in range(1, depth):
+            scales = receive(part, 2 + d)
+            total = total + decoded(came[part, base[2 + d]], scales)
+        out_ref[part] = total
+    for copy in copies.values():
         copy.wait_send()
 
 
@@ -283,38 +344,41 @@
         modes = mode_shapes.shape[-1]
         constants = tables()
         rows, columns = modes // axial, modes // circ
-        vmem = pl.BlockSpec(memory_space=pltpu.VMEM)
+        vmem, hbm = pl.BlockSpec(memory_space=pltpu.VMEM), pl.BlockSpec(memory_space=pltpu.HBM)
         scratch = [
             pltpu.VMEM((HALO, modes), jnp.float32),
             pltpu.VMEM((HALO_PAD, modes), jnp.float32),
             pltpu.SemaphoreType.DMA((5,)),
             pltpu.SemaphoreType.DMA((5,)),
             pltpu.VMEM((4 * PATCH, modes), jnp.bfloat16),
+            pltpu.VMEM(mode_shapes.shape, jnp.float32),
         ]
-        together = circ == 2 and axial % 4 == 0 and rows % 8 == 0 and columns % 128 == 0
+        scratch += [pltpu.VMEM(value.shape, jnp.bfloat16) for value in constants[:3]]
+        scratch.append(pltpu.SemaphoreType.DMA((7,)))
+        together = circ == 2 and axial % 4 == 0 and rows % 32 == 0 and columns % 128 == 0
         depth = axial // 4
         if together:
             kernel, shape = full_kernel, (2, rows, columns)
-            piece = (depth, 2, rows, columns)
+            steps, total = 2 + depth, 8 * depth
             scratch += [
-                pltpu.VMEM((2, 2, 2) + piece, jnp.float32),
-                pltpu.VMEM((2, 2) + piece, jnp.float32),
-                pltpu.VMEM((2,) + piece, jnp.float32),
-                pltpu.VMEM(piece, jnp.float32),
-                pltpu.VMEM((depth - 1,) + piece[1:], jnp.float32),
-                pltpu.SemaphoreType.DMA((2 + depth,)),
-                pltpu.SemaphoreType.DMA((2 + depth,)),
+                pltpu.VMEM((2, 8 * depth, rows, columns), jnp.float32),
+                pltpu.VMEM((2, total, rows, columns), jnp.int16),
+                pltpu.VMEM((2, total, rows, columns), jnp.int16),
+                pltpu.VMEM((2, steps, 8, columns), jnp.float32),
+                pltpu.VMEM((2, steps, 8, columns), jnp.float32),
+                pltpu.SemaphoreType.DMA((2, steps, 2)),
+                pltpu.SemaphoreType.DMA((2, steps, 2)),
             ]
         else:
             kernel, shape = plain_kernel, (2, modes, modes)
         result = pl.pallas_call(
             functools.partial(kernel, axial, circ),
             out_shape=jax.ShapeDtypeStruct(shape, jnp.float32),
-            in_specs=[vmem] * 8,
+            in_specs=[hbm] + [vmem] * 3 + [hbm] * 3 + [vmem],
             out_specs=vmem,
             scratch_shapes=scratch,
-            compiler_params=pltpu.CompilerParams(collective_id=0, has_side_effects=True, vmem_limit_bytes=40 * 1024 * 1024),
-        )(mode_shapes, amplitude, pair_list, pair_counts, *constants)
+            compiler_params=pltpu.CompilerParams(collective_id=0, has_side_effects=True, vmem_limit_bytes=56 * 1024 * 1024),
+        )(mode_shapes, amplitude, pair_list.reshape(3, 1, -1), pair_counts, *constants)
         if not together:
             result = lax.psum_scatter(result, "axial", scatter_dimension=1, tiled=True)
             result = lax.psum_scatter(result, "circ", scatter_dimension=2, tiled=True)

time: 40.7 us -> 29.9 us (0.73)
  Pallas kernels: 33.5 us -> 27.5 us
  local copies, waits for them, and re-layouts: 6.12 us -> 1.47 us
    pallas_call x1, Pallas kernels: 33.5 us -> 27.5 us  [body(): pl.pallas_call(functools.partial(kernel, axial, circ), out_shape=jax.Shap...]
    unnamed x16 -> x1, local copies, waits for them, and re-layouts: 6.12 us -> 1.47 us
where the time goes in v2:
time: 29.9 us; the launch traced here: 29.6 us
  Pallas kernels  27.5 us (92%)
  local copies, waits for them, and re-layouts  1.47 us (5%)
  between operations  0.66 us (2%)
    pallas_call x1, Pallas kernels, body(): pl.pallas_call(functools.partial(kernel, axial, circ), out_shape=jax.Shap...  27.5 us
    unnamed x1, local copies, waits for them, and re-layouts  1.47 us

profile of v2, /device:TPU:0, one launch (start us, length us, event | category | flops | bytes accessed | tf_op | source)
XLA Modules:
  0.0 29.6 jit_solution(18363858186666667916)
XLA Ops:
  0.7 27.5 %shard_map.82 = f32[2,32,256]{2,1,0:T(8,128)} custom-call(f32[2,2,128,512]{3,2,1,0:T(8,128)} %refs_0_.1, f32[2,2,128]{2,1,0:T(2,128)} %refs_1_.1, s32[3,1,20]{2,1,0:T(1,128)} %bitcast.1, s32[1,1]{1,0:T(1,128)S(6)} %copy.10.refs_3_, bf16[5,256,128]{2,1,0:T(8,128)(2,1)} %constant.8.clone.refs_4_, bf16[80,128]{1,0:T(8,128)(2,1)} %constant.9.clone.refs_5_, ...), custom_call_target="tpu_custom_call" | custom-call | tf_op jit(solution)/shard_map/pallas_call | solution.py:374
  28.2 1.5 %copy.11 = f32[2,32,256]{2,1,0:T(8,128)} copy(f32[2,32,256]{2,1,0:T(8,128)} %shard_map.82) | data formatting | bytes 131072

commit v3 on v2

--- a/solution.py
+++ b/solution.py
@@ -109,14 +109,15 @@
 
 
 def spectrum(axial, circ, operands, scratch, relations, deliver):
-    shapes_hbm, amp_ref, list_ref, count_ref, tiles_hbm, gather_hbm, spread_hbm, code_ref = operands
-    halo_out, halo_in, halo_send, halo_recv, weighted, shapes_ref, tiles_ref, gather_ref, spread_ref, fetch_sem = scratch
+    shapes_hbm, amp_hbm, list_hbm, count_hbm, tiles_hbm, gather_hbm, spread_hbm, code_hbm = operands
+    halo_out, halo_in, halo_send, halo_recv, weighted, shapes_ref, tiles_ref, gather_ref, spread_ref, amp_ref, list_ref, count_ref, code_ref, fetch_sem = scratch
     fetches = [
         pltpu.make_async_copy(source, target, fetch_sem.at[at])
         for at, (source, target) in enumerate(
             [(gather_hbm, gather_ref)]
             + [(shapes_hbm.at[block // 2, block % 2], shapes_ref.at[block // 2, block % 2]) for block in range(4)]
             + [(tiles_hbm, tiles_ref), (spread_hbm, spread_ref)]
+            + [(amp_hbm, amp_ref), (list_hbm, list_ref), (count_hbm, count_ref), (code_hbm, code_ref)]
         )
     ]
     for fetch in fetches:
@@ -129,12 +130,14 @@
 
     halo_in[...] = jnp.zeros_like(halo_in)
     barrier = pltpu.get_barrier_semaphore()
-    greeted = [device(sa, sc) for sa, sc, _, _ in MESSAGES] + [device(-sa, -sc) for sa, sc, _, _ in MESSAGES] + relations
+    steps = {(s * sa, s * sc % circ) for sa, sc, _, _ in MESSAGES for s in (1, -1)}
+    greeted = [device(sa, sc) for sa, sc in sorted(steps)] + relations
     for target in greeted:
         pl.semaphore_signal(barrier, inc=1, device_id=target, device_id_type=MESH)
 
     sums = []
     fetches[0].wait()
+    fetches[7].wait()
     for block in range(4):
         fetches[1 + block].wait()
         i, j = block // 2, block % 2
@@ -172,6 +175,8 @@
         for at in range(2, 5):
             copy_of(at).start()
 
+    for at in range(8, 11):
+        fetches[at].wait()
     slot_code = list_ref[0] * 5 + list_ref[1] * 3 + list_ref[2]
     kept = lax.broadcasted_iota(jnp.int32, slot_code.shape, 1) < count_ref[...]
     slot_code = jnp.where(kept, slot_code, -2)
@@ -251,8 +256,8 @@
 
 
 def full_kernel(axial, circ, *refs):
-    operands, out_ref, scratch = refs[:8], refs[8], refs[9:19]
-    pieces, sent, came, sent_scale, came_scale, send_sem, recv_sem = refs[19:]
+    operands, out_ref, scratch = refs[:8], refs[8], refs[9:23]
+    pieces, sent, came, sent_scale, came_scale, send_sem, recv_sem = refs[23:]
     a, c = lax.axis_index("axial"), lax.axis_index("circ")
     depth = axial // 4
     core, y, z = lax.rem(a, 2), lax.rem(a // 2, 2), a // 4
@@ -354,7 +359,14 @@
             pltpu.VMEM(mode_shapes.shape, jnp.float32),
         ]
         scratch += [pltpu.VMEM(value.shape, jnp.bfloat16) for value in constants[:3]]
-        scratch.append(pltpu.SemaphoreType.DMA((7,)))
+        listing = pair_list.reshape(3, 1, -1)
+        scratch += [
+            pltpu.VMEM(amplitude.shape, jnp.float32),
+            pltpu.VMEM(listing.shape, jnp.int32),
+            pltpu.VMEM((1, 1), jnp.int32),
+            pltpu.VMEM((HALO_PAD, 1), jnp.int32),
+            pltpu.SemaphoreType.DMA((11,)),
+        ]
         together = circ == 2 and axial % 4 == 0 and rows % 32 == 0 and columns % 128 == 0
         depth = axial // 4
         if together:
@@ -374,11 +386,11 @@
         result = pl.pallas_call(
             functools.partial(kernel, axial, circ),
             out_shape=jax.ShapeDtypeStruct(shape, jnp.float32),
-            in_specs=[hbm] + [vmem] * 3 + [hbm] * 3 + [vmem],
+            in_specs=[hbm] * 8,
             out_specs=vmem,
             scratch_shapes=scratch,
             compiler_params=pltpu.CompilerParams(collective_id=0, has_side_effects=True, vmem_limit_bytes=56 * 1024 * 1024),
-        )(mode_shapes, amplitude, pair_list.reshape(3, 1, -1), pair_counts, *constants)
+        )(mode_shapes, amplitude, listing, pair_counts, *constants)
         if not together:
             result = lax.psum_scatter(result, "axial", scatter_dimension=1, tiled=True)
             result = lax.psum_scatter(result, "circ", scatter_dimension=2, tiled=True)

time: 29.9 us -> 29 us (0.970)
  Pallas kernels: 27.5 us -> 26.7 us
    pallas_call x1, Pallas kernels: 27.5 us -> 26.7 us  [body(): pl.pallas_call(functools.partial(kernel, axial, circ), out_shape=jax.Shap...]
where the time goes in v3:
time: 29 us; the launch traced here: 28.9 us
  Pallas kernels  26.7 us (92%)
  local copies, waits for them, and re-layouts  1.47 us (5%)
  between operations  0.66 us (2%)
    pallas_call x1, Pallas kernels, body(): pl.pallas_call(functools.partial(kernel, axial, circ), out_shape=jax.Shap...  26.7 us
    unnamed x1, local copies, waits for them, and re-layouts  1.47 us

profile of v3, /device:TPU:0, one launch (start us, length us, event | category | flops | bytes accessed | tf_op | source)
XLA Modules:
  0.0 28.9 jit_solution(9336633742826514225)
XLA Ops:
  0.7 26.7 %shard_map.82 = f32[2,32,256]{2,1,0:T(8,128)} custom-call(f32[2,2,128,512]{3,2,1,0:T(8,128)} %refs_0_.1, f32[2,2,128]{2,1,0:T(2,128)} %refs_1_.1, s32[3,1,20]{2,1,0:T(1,128)} %bitcast.1, s32[1,1]{1,0:T(1,128)S(6)} %copy.10.refs_3_, bf16[5,256,128]{2,1,0:T(8,128)(2,1)} %constant.8.clone.refs_4_, bf16[80,128]{1,0:T(8,128)(2,1)} %constant.9.clone.refs_5_, ...), custom_call_target="tpu_custom_call" | custom-call | tf_op jit(solution)/shard_map/pallas_call | solution.py:386
  27.4 1.5 %copy.11 = f32[2,32,256]{2,1,0:T(8,128)} copy(f32[2,32,256]{2,1,0:T(8,128)} %shard_map.82) | data formatting | bytes 131072

commit v4 on v3

--- a/solution.py
+++ b/solution.py
@@ -248,11 +248,11 @@
     factor = LIMIT / most
     for at in range(count):
         write(at, jnp.round(read(at) * factor).astype(jnp.int32).astype(jnp.int16))
-    return jnp.broadcast_to(most * (1.0 / LIMIT), (8, most.shape[1]))
+    return most * (1.0 / LIMIT)
 
 
 def decoded(value, scales):
-    return value.astype(jnp.int32).astype(jnp.float32) * scales[0:1]
+    return value.astype(jnp.int32).astype(jnp.float32) * scales
 
 
 def full_kernel(axial, circ, *refs):
@@ -319,13 +319,15 @@
         own, give, keep = core * 4 * depth, (1 - key1) * 2 * depth, key1 * 2 * depth
         add(part, 0, scales, own, give, 2 * depth)
         send(part, 1, lambda at: pieces[part, own + give + at], 2 * depth, first)
-        add(part, 0, scales, own, keep, 2 * depth)
+    for part in range(2):
+        add(part, 0, came_scale[part, 0], own, keep, 2 * depth)
     for part in range(2):
         scales = receive(part, 1)
         own, give, keep = core * 4 * depth + key1 * 2 * depth, (1 - key2) * depth, key2 * depth
         add(part, 1, scales, own, give, depth)
         send(part, 2, lambda at: pieces[part, own + give + at], depth, second)
-        add(part, 1, scales, own, keep, depth)
+    for part in range(2):
+        add(part, 1, came_scale[part, 1], own, keep, depth)
     for part in range(2):
         scales = receive(part, 2)
         own = core * 4 * depth + key1 * 2 * depth + key2 * depth
@@ -376,8 +378,8 @@
                 pltpu.VMEM((2, 8 * depth, rows, columns), jnp.float32),
                 pltpu.VMEM((2, total, rows, columns), jnp.int16),
                 pltpu.VMEM((2, total, rows, columns), jnp.int16),
-                pltpu.VMEM((2, steps, 8, columns), jnp.float32),
-                pltpu.VMEM((2, steps, 8, columns), jnp.float32),
+                pltpu.VMEM((2, steps, 1, columns), jnp.float32),
+                pltpu.VMEM((2, steps, 1, columns), jnp.float32),
                 pltpu.SemaphoreType.DMA((2, steps, 2)),
                 pltpu.SemaphoreType.DMA((2, steps, 2)),
             ]

time: 29 us -> 27.9 us (0.962)
  Pallas kernels: 26.7 us -> 25.6 us
    pallas_call x1, Pallas kernels: 26.7 us -> 25.6 us  [body(): pl.pallas_call(functools.partial(kernel, axial, circ), out_shape=jax.Shap...]
where the time goes in v4:
time: 27.9 us; the launch traced here: 27.8 us
  Pallas kernels  25.6 us (92%)
  local copies, waits for them, and re-layouts  1.47 us (5%)
  between operations  0.66 us (2%)
    pallas_call x1, Pallas kernels, body(): pl.pallas_call(functools.partial(kernel, axial, circ), out_shape=jax.Shap...  25.6 us
    unnamed x1, local copies, waits for them, and re-layouts  1.47 us

profile of v4, /device:TPU:0, one launch (start us, length us, event | category | flops | bytes accessed | tf_op | source)
XLA Modules:
  0.0 27.8 jit_solution(1040765878884474226)
XLA Ops:
  0.7 25.6 %shard_map.82 = f32[2,32,256]{2,1,0:T(8,128)} custom-call(f32[2,2,128,512]{3,2,1,0:T(8,128)} %refs_0_.1, f32[2,2,128]{2,1,0:T(2,128)} %refs_1_.1, s32[3,1,20]{2,1,0:T(1,128)} %bitcast.1, s32[1,1]{1,0:T(1,128)S(6)} %copy.10.refs_3_, bf16[5,256,128]{2,1,0:T(8,128)(2,1)} %constant.8.clone.refs_4_, bf16[80,128]{1,0:T(8,128)(2,1)} %constant.9.clone.refs_5_, ...), custom_call_target="tpu_custom_call" | custom-call | tf_op jit(solution)/shard_map/pallas_call | solution.py:388
  26.3 1.5 %copy.11 = f32[2,32,256]{2,1,0:T(8,128)} copy(f32[2,32,256]{2,1,0:T(8,128)} %shard_map.82) | data formatting | bytes 131072

commit v5 on v4

--- a/solution.py
+++ b/solution.py
@@ -120,7 +120,7 @@
             + [(amp_hbm, amp_ref), (list_hbm, list_ref), (count_hbm, count_ref), (code_hbm, code_ref)]
         )
     ]
-    for fetch in fetches:
+    for fetch in fetches[7:] + fetches[:7]:
         fetch.start()
     a, c = lax.axis_index("axial"), lax.axis_index("circ")
     modes = weighted.shape[-1]

time: 27.9 us -> 27.8 us (level)
  no operation moved by 1% of the time
where the time goes in v5:
time: 27.8 us; the launch traced here: 27.6 us
  Pallas kernels  25.5 us (92%)
  local copies, waits for them, and re-layouts  1.47 us (5%)
  between operations  0.66 us (2%)
    pallas_call x1, Pallas kernels, body(): pl.pallas_call(functools.partial(kernel, axial, circ), out_shape=jax.Shap...  25.5 us
    unnamed x1, local copies, waits for them, and re-layouts  1.47 us

profile of v5, /device:TPU:0, one launch (start us, length us, event | category | flops | bytes accessed | tf_op | source)
XLA Modules:
  0.0 27.6 jit_solution(4347472819930499675)
XLA Ops:
  0.7 25.5 %shard_map.82 = f32[2,32,256]{2,1,0:T(8,128)} custom-call(f32[2,2,128,512]{3,2,1,0:T(8,128)} %refs_0_.1, f32[2,2,128]{2,1,0:T(2,128)} %refs_1_.1, s32[3,1,20]{2,1,0:T(1,128)} %bitcast.1, s32[1,1]{1,0:T(1,128)S(6)} %copy.10.refs_3_, bf16[5,256,128]{2,1,0:T(8,128)(2,1)} %constant.8.clone.refs_4_, bf16[80,128]{1,0:T(8,128)(2,1)} %constant.9.clone.refs_5_, ...), custom_call_target="tpu_custom_call" | custom-call | tf_op jit(solution)/shard_map/pallas_call | solution.py:388
  26.1 1.5 %copy.11 = f32[2,32,256]{2,1,0:T(8,128)} copy(f32[2,32,256]{2,1,0:T(8,128)} %shard_map.82) | data formatting | bytes 131072
